TPU v7x, 32 devices: a whole 2x2x4 slice. The times are simulated.
32 devices in a mesh: ax: 16 (over z, y, x), rad: 2 (over core).
Axes of the slice: x: 2, y: 2, z: 4, core: 2. Of those that a mesh axis runs over, the one named last changes fastest.
Arguments:
- fields: float32 [128, 5, 8, 1024], P('ax', None, None, 'rad'), may hold values from -6 to 6
Outputs:
- axial_deriv: float32 [128, 5, 8, 1024], P('ax', None, None, 'rad')
- filtered: float32 [128, 5, 8, 1024], P('ax', None, None, 'rad')
- radial_deriv: float32 [128, 5, 8, 1024], P('ax', None, None, 'rad')
All inputs are finite; a program needn't handle non-finite values.
Results may differ from a plain program's by a relative error of at most 0.0003.
Values sent between devices are 32-bit elements; how exact they have to be, the bound alone decides.
A program may use at most 128 MiB of HBM per device.

v0:
```python
import jax
import jax.numpy as jnp
from jax import lax
from jax.sharding import PartitionSpec as P

deriv_alpha = 1.0 / 3.0
filter_alpha = 0.4999
block_rows = 64


def with_halo(array, sides, width):
    for axis, dim in sides:
        size, length = (lax.axis_size(axis), array.shape[dim])
        up = [(i, (i + 1) % size) for i in range(size - 1)]
        down = [(j, i) for i, j in up]
        last = lax.slice_in_dim(array, length - width, length, axis=dim)
        initial = lax.slice_in_dim(array, 0, width, axis=dim)
        before = lax.ppermute(last, axis, up)
        after = lax.ppermute(initial, axis, down)
        array = jnp.concatenate([before, array, after], axis=dim)
    return array


def filter_weights():
    return [
        (93.0 + 70.0 * filter_alpha) / 128.0,
        (7.0 + 18.0 * filter_alpha) / 16.0,
        (-7.0 + 14.0 * filter_alpha) / 32.0,
        (1.0 - 2.0 * filter_alpha) / 16.0,
        (-1.0 + 2.0 * filter_alpha) / 128.0,
    ]


def sources(padded, count):

    def shifted(k):
        return padded[4 + k : 4 + k + count]

    deriv_rhs = 7.0 / 9.0 * (shifted(1) - shifted(-1)) + 1.0 / 36.0 * (shifted(2) - shifted(-2))
    weights = filter_weights()
    filter_rhs = weights[0] * shifted(0)
    for n in range(1, 5):
        filter_rhs = filter_rhs + weights[n] / 2.0 * (shifted(n) + shifted(-n))
    return jnp.stack([deriv_rhs, filter_rhs])


def pivots(alpha, rows):
    root = (1.0 - 4.0 * alpha * alpha) ** 0.5
    big_root = (1.0 + root) / 2.0
    ratio = (1.0 - root) / (1.0 + root)
    return big_root * (1.0 - jnp.power(ratio, rows + 2.0)) / (1.0 - jnp.power(ratio, rows + 1.0))


def tables(alpha, rows):
    length = rows.shape[-1]
    piv = pivots(alpha, rows)
    before = pivots(alpha, jnp.maximum(rows - 1.0, 0.0))
    log_fwd = jnp.log(alpha / before)
    cum_fwd = jnp.cumsum(log_fwd, axis=-1)
    log_bwd = jnp.log(alpha / piv)
    cum_bwd = jnp.cumsum(log_bwd, axis=-1)
    excl_bwd = cum_bwd - log_bwd
    index = jnp.arange(length)
    parity = ((index[:, None] - index[None, :]) % 2).astype(jnp.float32)
    signs = 1.0 - 2.0 * parity
    lower = index[:, None] >= index[None, :]
    upper = index[:, None] <= index[None, :]
    diff_fwd = jnp.minimum(cum_fwd[..., :, None] - cum_fwd[..., None, :], 0.0)
    forward = jnp.where(lower, signs * jnp.exp(diff_fwd), 0.0)
    diff_bwd = jnp.minimum(excl_bwd[..., None, :] - excl_bwd[..., :, None], 0.0)
    backward = jnp.where(upper, signs * jnp.exp(diff_bwd) / piv[..., None, :], 0.0)
    sign_in = 1.0 - 2.0 * ((index + 1) % 2).astype(jnp.float32)
    gain_in = sign_in * jnp.exp(cum_fwd)
    sign_out = 1.0 - 2.0 * ((length - index) % 2).astype(jnp.float32)
    gain_out = sign_out * jnp.exp(cum_bwd[..., length - 1 :] - excl_bwd)
    return (forward, gain_in, backward, gain_out)


def combine(earlier, later):
    return (earlier[0] * later[0], later[1] + later[0] * earlier[1])


def solve(rhs, rows, chain_forward, chain_backward):
    parts = [tables(deriv_alpha, rows), tables(filter_alpha, rows)]
    forward = jnp.stack([parts[0][0], parts[1][0]])
    gain_in = jnp.stack([parts[0][1], parts[1][1]])
    backward = jnp.stack([parts[0][2], parts[1][2]])
    gain_out = jnp.stack([parts[0][3], parts[1][3]])
    local_fwd = jnp.einsum("sbkj,sbjl->sbkl", forward, rhs, precision=lax.Precision.HIGHEST)
    incoming = chain_forward(gain_in[:, :, -1:], local_fwd[:, :, -1, :])
    eliminated = local_fwd + gain_in[..., None] * incoming[:, :, None, :]
    local_bwd = jnp.einsum("sbkj,sbjl->sbkl", backward, eliminated, precision=lax.Precision.HIGHEST)
    outgoing = chain_backward(gain_out[:, :, :1], local_bwd[:, :, 0, :])
    return local_bwd + gain_out[..., None] * outgoing[:, :, None, :]


def block_chain(coeff, offset):
    inclusive = lax.associative_scan(combine, (coeff, offset), axis=1)
    return jnp.concatenate([jnp.zeros_like(offset[:, :1]), inclusive[1][:, :-1]], axis=1)


def block_forward(coeff, offset):
    return block_chain(coeff, offset)


def block_backward(coeff, offset):
    flipped = block_chain(jnp.flip(coeff, axis=1), jnp.flip(offset, axis=1))
    return jnp.flip(flipped, axis=1)


def body(fields):
    rows_dev, count, planes, radial = fields.shape
    width = count * planes * radial
    rimmed = with_halo(fields, (("rad", 3),), 3)

    def radial_cell(k):
        return rimmed[:, :, :, 3 + k : 3 + k + radial]

    radial_deriv = (
        45.0 * (radial_cell(1) - radial_cell(-1))
        - 9.0 * (radial_cell(2) - radial_cell(-2))
        + (radial_cell(3) - radial_cell(-3))
    ) / 60.0
    flat = fields.reshape(rows_dev, width)
    lines = lax.all_to_all(flat, "ax", split_axis=1, concat_axis=0, tiled=True)
    total = lines.shape[0]
    padded = jnp.pad(lines, ((4, 4), (0, 0)))
    rhs = sources(padded, total)
    blocks = total // block_rows
    rows = jnp.arange(total, dtype=jnp.float32).reshape(blocks, block_rows)
    solved = solve(rhs.reshape(2, blocks, block_rows, -1), rows, block_forward, block_backward)
    solved = solved.reshape(2, total, -1)
    result = lax.all_to_all(solved, "ax", split_axis=1, concat_axis=2, tiled=True)
    axial_deriv = result[0].reshape(fields.shape)
    filtered = result[1].reshape(fields.shape)
    return (axial_deriv, filtered, radial_deriv)


def solution(mesh):
    in_specs = (P("ax", None, None, "rad"),)
    out_specs = (P("ax", None, None, "rad"), P("ax", None, None, "rad"), P("ax", None, None, "rad"))
    return jax.shard_map(body, mesh=mesh, in_specs=in_specs, out_specs=out_specs, check_vma=False)
```

profile of v0, /device:TPU:8, one launch (start us, length us, event | category | flops | bytes accessed | tf_op | source)
XLA Modules:
  0.0 72.5 jit_solution(13071631974729192661)
XLA Ops:
  0.6 1.3 %all_to_all.25 = f32[8,16,1280]{2,1,0:T(8,128)S(1)} reshape(f32[8,5,8,512]{3,2,1,0:T(8,128)} %param.1) | data formatting | bytes 1310720 | tf_op jit(solution)/shard_map/all_to_all | solution.py:125
  1.9 1.2 %copy.11 = f32[8,16,1280]{2,0,1:T(8,128)} copy(f32[8,16,1280]{2,1,0:T(8,128)S(1)} %all_to_all.25) | data formatting | bytes 1310720 | tf_op jit(solution)/shard_map/all_to_all | solution.py:125
  3.2 7.2 %all-to-all-start = ((f32[8,16,1280]{2,0,1:T(8,128)}), f32[8,16,1280]{2,0,1:T(8,128)S(1)}, u32[]{:S(2)}, u32[]{:S(2)}) async-start(f32[8,16,1280]{2,0,1:T(8,128)} %copy.11), calls=%async_computation | async-start | bytes 1310720 | tf_op jit(solution)/shard_map/all_to_all | solution.py:125
  10.5 0.2 reduce_window_sum.36
  10.8 0.2 reduce_window_sum.29
  11.0 0.2 reduce_window_sum.28
  11.3 0.2 reduce_window_sum.27
  11.5 0.2 slice_reduce_fusion
  11.7 0.1 fusion.39
  11.8 0.1 fusion.49
  11.9 0.2 fusion.48
  12.2 0.1 divide_select_fusion.1
  12.4 15.2 %all-to-all-done = f32[8,16,1280]{2,0,1:T(8,128)S(1)} async-done(((f32[8,16,1280]{2,0,1:T(8,128)}), f32[8,16,1280]{2,0,1:T(8,128)S(1)}, u32[]{:S(2)}, u32[]{:S(2)}) %all-to-all-start) | async-done | bytes 655392 | tf_op jit(solution)/shard_map/all_to_all | solution.py:125
  27.6 0.7 multiply_add_fusion.2
  28.3 1.2 %fusion = f32[2,2,64,1280]{3,2,1,0:T(8,128)S(1)} fusion(f32[1,2,64,1280]{3,2,1,0:T(8,128)S(1)} %bitcast.45, f32[1,2,64,1280]{3,2,1,0:T(8,128)S(1)} %bitcast.44, f32[1,2,64,64]{3,2,1,0:T(8,128)S(1)} %get-tuple-element.13, f32[1,2,64,64]{3,2,1,0:T(8,128)S(1)} %get-tuple-element.14), kind=kOutput, calls=%fused_computation | convolution fusion | flops 252002304 | bytes 2686976 | tf_op jit(solution)/shard_map/sbkj,sbjl->sbkl/dot_general | solution.py:89
  29.6 0.1 fusion.67
  29.7 1.3 %fusion.4 = f32[2,2,64,1280]{3,2,1,0:T(8,128)S(1)} fusion(f32[2,2,64,1280]{3,2,1,0:T(8,128)S(1)} %fusion, f32[2,2,1280]{2,1,0:T(2,128)S(1)} %concatenate.18, f32[2,2,64]{2,1,0:T(2,128)S(1)} %pad_maximum_fusion.1, f32[1,2,64,64]{3,2,1,0:T(8,128)S(1)} %get-tuple-element.10, f32[1,2,64,64]{3,2,1,0:T(8,128)S(1)} %get-tuple-element.9), kind=kOutput, calls=%fused_computation.5 | convolution fusion | flops 252329984 | bytes 2708480 | tf_op jit(solution)/shard_map/sbkj,sbjl->sbkl/dot_general | solution.py:92
  31.0 0.1 fusion.66
  31.2 0.3 rev.7
  31.5 0.2 multiply_add_fusion
  31.6 2.1 %copy.12 = f32[2,128,1280]{2,0,1:T(2,128)} copy(f32[2,128,1280]{2,1,0:T(8,128)S(1)} %bitcast.42) | data formatting | bytes 2621440 | tf_op jit(solution)/shard_map/reshape | solution.py:132
  33.7 0.0 copy-start
  33.7 4.8 %all-to-all-start.1 = ((f32[2,128,1280]{2,0,1:T(2,128)}), f32[2,128,1280]{2,0,1:T(2,128)S(1)}, u32[]{:S(2)}, u32[]{:S(2)}) async-start(f32[2,128,1280]{2,0,1:T(2,128)} %copy.12), calls=%async_computation.1 | async-start | bytes 2621440 | tf_op jit(solution)/shard_map/all_to_all | solution.py:133
  38.5 0.0 copy-done
  38.5 0.1 fusion.65
  38.6 1.3 %collective-permute-start = (f32[8,5,8,3]{3,2,1,0:T(8,128)S(1)}, f32[8,5,8,3]{3,2,1,0:T(8,128)S(1)}, u32[]{:S(2)}, u32[]{:S(2)}) collective-permute-start(f32[8,5,8,3]{3,2,1,0:T(8,128)S(1)} %get-tuple-element.5), channel_id=1, source_target_pairs={{1,0},{3,2},{5,4},{7,6},{9,8},{11,10},{13,12},{15,14},{17,16},{19,... | collective-permute-start | bytes 11528 | tf_op jit(solution)/shard_map/ppermute | solution.py:19
  39.9 3.0 %collective-permute-start.1 = (f32[8,5,8,3]{3,2,1,0:T(8,128)S(1)}, f32[8,5,8,3]{3,2,1,0:T(8,128)S(1)}, u32[]{:S(2)}, u32[]{:S(2)}) collective-permute-start(f32[8,5,8,3]{3,2,1,0:T(8,128)S(1)} %get-tuple-element.6), channel_id=1, source_target_pairs={{0,1},{2,3},{4,5},{6,7},{8,9},{10,11},{12,13},{14,15},{16,17},{18,... | collective-permute-start | bytes 11528 | tf_op jit(solution)/shard_map/ppermute | solution.py:18
  43.0 0.0 collective-permute-done
  43.0 0.9 %collective-permute-done.1 = f32[8,5,8,3]{3,2,1,0:T(8,128)S(1)} collective-permute-done((f32[8,5,8,3]{3,2,1,0:T(8,128)S(1)}, f32[8,5,8,3]{3,2,1,0:T(8,128)S(1)}, u32[]{:S(2)}, u32[]{:S(2)}) %collective-permute-start.1) | collective-permute-done | bytes 3872 | tf_op jit(solution)/shard_map/ppermute | solution.py:18
  44.0 2.0 %fusion.12 = f32[8,5,8,512]{3,2,1,0:T(8,128)} fusion(f32[8,5,8,512]{3,2,1,0:T(8,128)S(1)} %copy-done, f32[8,5,8,3]{3,2,1,0:T(8,128)S(1)} %collective-permute-done.1, f32[8,5,8,515]{3,2,1,0:T(8,128)S(1)} %constant_dynamic-update-slice_fusion), kind=kLoop, calls=%fused_computation.17 | loop fusion | flops 1802240 | bytes 3280640 | tf_op jit(solution)/shard_map/div | solution.py:119
  46.0 23.0 %all-to-all-done.1 = f32[2,128,1280]{2,0,1:T(2,128)S(1)} async-done(((f32[2,128,1280]{2,0,1:T(2,128)}), f32[2,128,1280]{2,0,1:T(2,128)S(1)}, u32[]{:S(2)}, u32[]{:S(2)}) %all-to-all-start.1) | async-done | bytes 1310752 | tf_op jit(solution)/shard_map/all_to_all | solution.py:133
  69.0 1.0 %fusion.64 = (f32[1,8,16,1280]{3,0,1,2:T(1,128)S(1)}, f32[1,8,16,1280]{3,0,1,2:T(1,128)S(1)}) fusion(f32[2,8,16,1280]{3,0,1,2:T(2,128)S(1)} %bitcast.41), kind=kLoop, calls=%fused_computation.122 | loop fusion | bytes 2621440 | tf_op jit(solution)/shard_map/slice | solution.py:135
  70.0 0.2 copy.14
  70.3 1.0 %reshape_squeeze.7 = f32[8,5,8,512]{3,2,1,0:T(8,128)} reshape(f32[1,8,16,1280]{3,2,1,0:T(8,128)S(1)} %copy.14) | data formatting | bytes 1310720 | tf_op jit(solution)/shard_map/reshape;squeeze | solution.py:135
  71.3 0.2 copy.13
  71.5 1.0 %reshape_squeeze.6 = f32[8,5,8,512]{3,2,1,0:T(8,128)} reshape(f32[1,8,16,1280]{3,2,1,0:T(8,128)S(1)} %copy.13) | data formatting | bytes 1310720 | tf_op jit(solution)/shard_map/reshape;squeeze | solution.py:134
  (23 shorter events, 0.4 us)
Async XLA Ops:
  3.2 24.4 %all-to-all-start = ((f32[8,16,1280]{2,0,1:T(8,128)}), f32[8,16,1280]{2,0,1:T(8,128)S(1)}, u32[]{:S(2)}, u32[]{:S(2)}) async-start(f32[8,16,1280]{2,0,1:T(8,128)} %copy.11), calls=%async_computation | async-start | bytes 1310720 | tf_op jit(solution)/shard_map/all_to_all | solution.py:125
  33.7 4.8 %copy-start = (f32[8,5,8,512]{3,2,1,0:T(8,128)S(1)}, f32[8,5,8,512]{3,2,1,0:T(8,128)}, u32[]{:S(2)}) copy-start(f32[8,5,8,512]{3,2,1,0:T(8,128)} %param.1) | copy-start | bytes 1966084
  33.7 35.3 %all-to-all-start.1 = ((f32[2,128,1280]{2,0,1:T(2,128)}), f32[2,128,1280]{2,0,1:T(2,128)S(1)}, u32[]{:S(2)}, u32[]{:S(2)}) async-start(f32[2,128,1280]{2,0,1:T(2,128)} %copy.12), calls=%async_computation.1 | async-start | bytes 2621440 | tf_op jit(solution)/shard_map/all_to_all | solution.py:133
  38.6 4.4 %collective-permute-start = (f32[8,5,8,3]{3,2,1,0:T(8,128)S(1)}, f32[8,5,8,3]{3,2,1,0:T(8,128)S(1)}, u32[]{:S(2)}, u32[]{:S(2)}) collective-permute-start(f32[8,5,8,3]{3,2,1,0:T(8,128)S(1)} %get-tuple-element.5), channel_id=1, source_target_pairs={{1,0},{3,2},{5,4},{7,6},{9,8},{11,10},{13,12},{15,14},{17,16},{19,... | collective-permute-start | bytes 11528 | tf_op jit(solution)/shard_map/ppermute | solution.py:19
  39.9 4.1 %collective-permute-start.1 = (f32[8,5,8,3]{3,2,1,0:T(8,128)S(1)}, f32[8,5,8,3]{3,2,1,0:T(8,128)S(1)}, u32[]{:S(2)}, u32[]{:S(2)}) collective-permute-start(f32[8,5,8,3]{3,2,1,0:T(8,128)S(1)} %get-tuple-element.6), channel_id=1, source_target_pairs={{0,1},{2,3},{4,5},{6,7},{8,9},{10,11},{12,13},{14,15},{16,17},{18,... | collective-permute-start | bytes 11528 | tf_op jit(solution)/shard_map/ppermute | solution.py:18
where the time goes:
time: 72.9 us; the launch traced here: 72.5 us
  waiting for transfers between devices  39.2 us (54%)
  starting transfers between devices  16.3 us (22%)
  local copies, waits for them, and re-layouts  8.85 us (12%)
  other arithmetic  4.78 us (7%)
  matrix products  2.54 us (3%)
  between operations  0.86 us (1%)
    all_to_all x1, waiting for transfers between devices, body(): lax.all_to_all(solved, 'ax', split_axis=1, concat_axis=2, tiled=True)  23 us
    all_to_all x1, waiting for transfers between devices, body(): lines = lax.all_to_all(flat, 'ax', split_axis=1, concat_axis=0, tiled=True)  15.2 us
    all_to_all x1, starting transfers between devices, body(): lines = lax.all_to_all(flat, 'ax', split_axis=1, concat_axis=0, tiled=True)  7.22 us
    all_to_all x1, starting transfers between devices, body(): lax.all_to_all(solved, 'ax', split_axis=1, concat_axis=2, tiled=True)  4.77 us
    ppermute x1, starting transfers between devices, with_halo(): before = lax.ppermute(last, axis, up)  3.05 us
    all_to_all x2, local copies, waits for them, and re-layouts, body(): lines = lax.all_to_all(flat, 'ax', split_axis=1, concat_axis=0, tiled=True)  2.53 us
    reshape x1, local copies, waits for them, and re-layouts, body(): solved = solved.reshape(2, total, -1)  2.07 us
    div x1, other arithmetic, body(): (45.0 * (radial_cell(1) - radial_cell(-1)) - 9.0 * (radial_cell(2) - radi...  2.02 us
  transfers between devices with their start and end apart: 4, of which 3 were waited for; matrix products, arithmetic and copies ran while one was open for 6% of the time, Pallas kernels for 0%

commit v1 on v0

--- a/solution.py
+++ b/solution.py
@@ -122,7 +122,15 @@
         + (radial_cell(3) - radial_cell(-3))
     ) / 60.0
     flat = fields.reshape(rows_dev, width)
-    lines = lax.all_to_all(flat, "ax", split_axis=1, concat_axis=0, tiled=True)
+
+    def define_the_tracks(local_x, axis_key):
+        local_next = lax.axis_size(axis_key)
+        w1 = jnp.split(local_x, local_next, axis=1)
+        local_now = jnp.stack(w1)
+        state_next = lax.all_to_all(local_now, axis_key, 0, 0)
+        return jnp.concatenate(state_next, axis=0)
+
+    lines = define_the_tracks(flat, "ax")
     total = lines.shape[0]
     padded = jnp.pad(lines, ((4, 4), (0, 0)))
     rhs = sources(padded, total)

time: 72.9 us -> 81.8 us (1.12)
  local copies, waits for them, and re-layouts: 8.85 us -> 17.7 us
    unnamed x5 -> x21, local copies, waits for them, and re-layouts: 0.07 us -> 10.8 us
    all_to_all x2 -> x0, local copies, waits for them, and re-layouts: 2.53 us -> none  [body(): lines = lax.all_to_all(flat, 'ax', split_axis=1, concat_axis=0, tiled=True)]
  transfers between devices with their start and end apart: 4 -> 4, of which waited for: 3 -> 3; matrix products, arithmetic and copies ran while one was open for 6% -> 5% of each run, Pallas kernels for 0% -> 0%
where the time goes in v1:
time: 81.8 us; the launch traced here: 81.4 us
  waiting for transfers between devices  39.2 us (48%)
  local copies, waits for them, and re-layouts  17.7 us (22%)
  starting transfers between devices  16.3 us (20%)
  other arithmetic  4.78 us (6%)
  matrix products  2.53 us (3%)
  between operations  0.87 us (1%)
    all_to_all x1, waiting for transfers between devices, body(): lax.all_to_all(solved, 'ax', split_axis=1, concat_axis=2, tiled=True)  23 us
    all_to_all x1, waiting for transfers between devices, define_the_tracks(): state_next = lax.all_to_all(local_now, axis_key, 0, 0)  15.2 us
    unnamed x21, local copies, waits for them, and re-layouts  10.8 us
    all_to_all x1, starting transfers between devices, define_the_tracks(): state_next = lax.all_to_all(local_now, axis_key, 0, 0)  7.22 us
    all_to_all x1, starting transfers between devices, body(): lax.all_to_all(solved, 'ax', split_axis=1, concat_axis=2, tiled=True)  4.78 us
    ppermute x1, starting transfers between devices, with_halo(): before = lax.ppermute(last, axis, up)  3.05 us
    reshape x1, local copies, waits for them, and re-layouts, body(): solved = solved.reshape(2, total, -1)  2.07 us
    div x1, other arithmetic, body(): (45.0 * (radial_cell(1) - radial_cell(-1)) - 9.0 * (radial_cell(2) - radi...  2.02 us
  transfers between devices with their start and end apart: 4, of which 3 were waited for; matrix products, arithmetic and copies ran while one was open for 5% of the time, Pallas kernels for 0%

profile of v1, /device:TPU:8, one launch (start us, length us, event | category | flops | bytes accessed | tf_op | source)
XLA Modules:
  0.0 81.4 jit_solution(4989583152934408210)
XLA Ops:
  0.6 1.5 %copy.11 = f32[1,8,40,512]{3,1,2,0:T(8,128)S(1)} copy(f32[1,8,40,512]{3,2,1,0:T(8,128)} %bitcast.104) | data formatting | bytes 1310720
  2.1 0.6 fusion.40
  2.7 0.6 fusion.39
  3.3 0.6 fusion.38
  4.0 0.6 fusion.37
  4.6 0.6 fusion.36
  5.2 0.6 fusion.35
  5.8 0.6 fusion.34
  6.4 0.6 fusion.33
  7.1 0.6 fusion.32
  7.7 0.6 fusion.31
  8.3 0.6 fusion.30
  8.9 0.6 fusion.29
  9.6 0.6 fusion.28
  10.2 0.6 fusion.27
  10.8 0.6 fusion.26
  11.4 0.6 fusion.25
  12.0 7.2 %all-to-all-start = ((f32[16,8,1280]{2,1,0:T(8,128)}), f32[16,8,1280]{2,1,0:T(8,128)S(1)}, u32[]{:S(2)}, u32[]{:S(2)}) async-start(f32[16,8,1280]{2,1,0:T(8,128)} %fusion.25), calls=%async_computation | async-start | bytes 1310720 | tf_op jit(solution)/shard_map/all_to_all | solution.py:130
  19.4 0.2 reduce_window_sum.36
  19.7 0.2 reduce_window_sum.29
  19.9 0.2 reduce_window_sum.28
  20.1 0.2 reduce_window_sum.27
  20.4 0.2 slice_reduce_fusion
  20.6 0.1 fusion.55
  20.7 0.1 fusion.65
  20.8 0.2 fusion.64
  21.1 0.1 divide_select_fusion.1
  21.3 15.2 %all-to-all-done = f32[16,8,1280]{2,1,0:T(8,128)S(1)} async-done(((f32[16,8,1280]{2,1,0:T(8,128)}), f32[16,8,1280]{2,1,0:T(8,128)S(1)}, u32[]{:S(2)}, u32[]{:S(2)}) %all-to-all-start) | async-done | bytes 655392 | tf_op jit(solution)/shard_map/all_to_all | solution.py:130
  36.5 0.7 multiply_add_fusion.2
  37.1 1.2 %fusion = f32[2,2,64,1280]{3,2,1,0:T(8,128)S(1)} fusion(f32[1,2,64,1280]{3,2,1,0:T(8,128)S(1)} %bitcast.109, f32[1,2,64,1280]{3,2,1,0:T(8,128)S(1)} %bitcast.108, f32[1,2,64,64]{3,2,1,0:T(8,128)S(1)} %get-tuple-element.13, f32[1,2,64,64]{3,2,1,0:T(8,128)S(1)} %get-tuple-element.14), kind=kOutput, calls=%fused_computation | convolution fusion | flops 252002304 | bytes 2686976 | tf_op jit(solution)/shard_map/sbkj,sbjl->sbkl/dot_general | solution.py:89
  38.4 0.1 fusion.83
  38.5 1.3 %fusion.4 = f32[2,2,64,1280]{3,2,1,0:T(8,128)S(1)} fusion(f32[2,2,64,1280]{3,2,1,0:T(8,128)S(1)} %fusion, f32[2,2,1280]{2,1,0:T(2,128)S(1)} %concatenate.18, f32[2,2,64]{2,1,0:T(2,128)S(1)} %pad_maximum_fusion.1, f32[1,2,64,64]{3,2,1,0:T(8,128)S(1)} %get-tuple-element.10, f32[1,2,64,64]{3,2,1,0:T(8,128)S(1)} %get-tuple-element.9), kind=kOutput, calls=%fused_computation.5 | convolution fusion | flops 252329984 | bytes 2708480 | tf_op jit(solution)/shard_map/sbkj,sbjl->sbkl/dot_general | solution.py:92
  39.9 0.1 fusion.82
  40.0 0.3 rev.7
  40.3 0.2 multiply_add_fusion
  40.5 2.1 %copy.6 = f32[2,128,1280]{2,0,1:T(2,128)} copy(f32[2,128,1280]{2,1,0:T(8,128)S(1)} %bitcast.106) | data formatting | bytes 2621440 | tf_op jit(solution)/shard_map/reshape | solution.py:140
  42.6 0.0 copy-start
  42.6 4.8 %all-to-all-start.1 = ((f32[2,128,1280]{2,0,1:T(2,128)}), f32[2,128,1280]{2,0,1:T(2,128)S(1)}, u32[]{:S(2)}, u32[]{:S(2)}) async-start(f32[2,128,1280]{2,0,1:T(2,128)} %copy.6), calls=%async_computation.1 | async-start | bytes 2621440 | tf_op jit(solution)/shard_map/all_to_all | solution.py:141
  47.4 0.0 copy-done
  47.4 0.1 fusion.81
  47.5 1.3 %collective-permute-start = (f32[8,5,8,3]{3,2,1,0:T(8,128)S(1)}, f32[8,5,8,3]{3,2,1,0:T(8,128)S(1)}, u32[]{:S(2)}, u32[]{:S(2)}) collective-permute-start(f32[8,5,8,3]{3,2,1,0:T(8,128)S(1)} %get-tuple-element.5), channel_id=1, source_target_pairs={{1,0},{3,2},{5,4},{7,6},{9,8},{11,10},{13,12},{15,14},{17,16},{19,... | collective-permute-start | bytes 11528 | tf_op jit(solution)/shard_map/ppermute | solution.py:19
  48.8 3.0 %collective-permute-start.1 = (f32[8,5,8,3]{3,2,1,0:T(8,128)S(1)}, f32[8,5,8,3]{3,2,1,0:T(8,128)S(1)}, u32[]{:S(2)}, u32[]{:S(2)}) collective-permute-start(f32[8,5,8,3]{3,2,1,0:T(8,128)S(1)} %get-tuple-element.6), channel_id=1, source_target_pairs={{0,1},{2,3},{4,5},{6,7},{8,9},{10,11},{12,13},{14,15},{16,17},{18,... | collective-permute-start | bytes 11528 | tf_op jit(solution)/shard_map/ppermute | solution.py:18
  51.9 0.0 collective-permute-done
  51.9 0.9 %collective-permute-done.1 = f32[8,5,8,3]{3,2,1,0:T(8,128)S(1)} collective-permute-done((f32[8,5,8,3]{3,2,1,0:T(8,128)S(1)}, f32[8,5,8,3]{3,2,1,0:T(8,128)S(1)}, u32[]{:S(2)}, u32[]{:S(2)}) %collective-permute-start.1) | collective-permute-done | bytes 3872 | tf_op jit(solution)/shard_map/ppermute | solution.py:18
  52.8 2.0 %fusion.12 = f32[8,5,8,512]{3,2,1,0:T(8,128)} fusion(f32[8,5,8,512]{3,2,1,0:T(8,128)S(1)} %copy-done, f32[8,5,8,3]{3,2,1,0:T(8,128)S(1)} %collective-permute-done.1, f32[8,5,8,515]{3,2,1,0:T(8,128)S(1)} %constant_dynamic-update-slice_fusion), kind=kLoop, calls=%fused_computation.17 | loop fusion | flops 1802240 | bytes 3280640 | tf_op jit(solution)/shard_map/div | solution.py:119
  54.9 23.0 %all-to-all-done.1 = f32[2,128,1280]{2,0,1:T(2,128)S(1)} async-done(((f32[2,128,1280]{2,0,1:T(2,128)}), f32[2,128,1280]{2,0,1:T(2,128)S(1)}, u32[]{:S(2)}, u32[]{:S(2)}) %all-to-all-start.1) | async-done | bytes 1310752 | tf_op jit(solution)/shard_map/all_to_all | solution.py:141
  77.9 1.0 %fusion.80 = (f32[1,8,16,1280]{3,0,1,2:T(1,128)S(1)}, f32[1,8,16,1280]{3,0,1,2:T(1,128)S(1)}) fusion(f32[2,8,16,1280]{3,0,1,2:T(2,128)S(1)} %bitcast.105), kind=kLoop, calls=%fused_computation.154 | loop fusion | bytes 2621440 | tf_op jit(solution)/shard_map/slice | solution.py:143
  78.9 0.2 copy.8
  79.1 1.0 %reshape_squeeze.7 = f32[8,5,8,512]{3,2,1,0:T(8,128)} reshape(f32[1,8,16,1280]{3,2,1,0:T(8,128)S(1)} %copy.8) | data formatting | bytes 1310720 | tf_op jit(solution)/shard_map/reshape;squeeze | solution.py:143
  80.2 0.2 copy.7
  80.4 1.0 %reshape_squeeze.6 = f32[8,5,8,512]{3,2,1,0:T(8,128)} reshape(f32[1,8,16,1280]{3,2,1,0:T(8,128)S(1)} %copy.7) | data formatting | bytes 1310720 | tf_op jit(solution)/shard_map/reshape;squeeze | solution.py:142
  (23 shorter events, 0.4 us)
Async XLA Ops:
  12.0 24.4 %all-to-all-start = ((f32[16,8,1280]{2,1,0:T(8,128)}), f32[16,8,1280]{2,1,0:T(8,128)S(1)}, u32[]{:S(2)}, u32[]{:S(2)}) async-start(f32[16,8,1280]{2,1,0:T(8,128)} %fusion.25), calls=%async_computation | async-start | bytes 1310720 | tf_op jit(solution)/shard_map/all_to_all | solution.py:130
  42.6 4.8 %copy-start = (f32[8,5,8,512]{3,2,1,0:T(8,128)S(1)}, f32[8,5,8,512]{3,2,1,0:T(8,128)}, u32[]{:S(2)}) copy-start(f32[8,5,8,512]{3,2,1,0:T(8,128)} %param.1) | copy-start | bytes 1966084
  42.6 35.3 %all-to-all-start.1 = ((f32[2,128,1280]{2,0,1:T(2,128)}), f32[2,128,1280]{2,0,1:T(2,128)S(1)}, u32[]{:S(2)}, u32[]{:S(2)}) async-start(f32[2,128,1280]{2,0,1:T(2,128)} %copy.6), calls=%async_computation.1 | async-start | bytes 2621440 | tf_op jit(solution)/shard_map/all_to_all | solution.py:141
  47.5 4.4 %collective-permute-start = (f32[8,5,8,3]{3,2,1,0:T(8,128)S(1)}, f32[8,5,8,3]{3,2,1,0:T(8,128)S(1)}, u32[]{:S(2)}, u32[]{:S(2)}) collective-permute-start(f32[8,5,8,3]{3,2,1,0:T(8,128)S(1)} %get-tuple-element.5), channel_id=1, source_target_pairs={{1,0},{3,2},{5,4},{7,6},{9,8},{11,10},{13,12},{15,14},{17,16},{19,... | collective-permute-start | bytes 11528 | tf_op jit(solution)/shard_map/ppermute | solution.py:19
  48.8 4.1 %collective-permute-start.1 = (f32[8,5,8,3]{3,2,1,0:T(8,128)S(1)}, f32[8,5,8,3]{3,2,1,0:T(8,128)S(1)}, u32[]{:S(2)}, u32[]{:S(2)}) collective-permute-start(f32[8,5,8,3]{3,2,1,0:T(8,128)S(1)} %get-tuple-element.6), channel_id=1, source_target_pairs={{0,1},{2,3},{4,5},{6,7},{8,9},{10,11},{12,13},{14,15},{16,17},{18,... | collective-permute-start | bytes 11528 | tf_op jit(solution)/shard_map/ppermute | solution.py:18
